TPU v7x, 32 devices: a whole 2x2x4 slice. The times are simulated.
32 devices in a mesh: groups: 2 (over x), section: 4 (over z), seq: 4 (over y, core).
Axes of the slice: x: 2, y: 2, z: 4, core: 2. Of those that a mesh axis runs over, the one named last changes fastest.
Arguments:
- queries: bfloat16 [2048, 4096], P(('groups', 'section', 'seq')), parts along dimension 0, may hold values from -6 to 6
- keys: bfloat16 [2048, 4096], P(('groups', 'section', 'seq')), parts along dimension 0, may hold values from -6 to 6
- values: bfloat16 [2048, 4096], P(('groups', 'section', 'seq')), parts along dimension 0, may hold values from -6 to 6
- query_gain: float32 [4096], replicated, may hold values from 0.1 to 1.9
- key_gain: float32 [4096], replicated, may hold values from 0.1 to 1.9
- placement: int32 [8], P('groups'), parts along dimension 0, may hold values from 0 to 3, each once
- span_mask: int32 [8, 4], P('groups'), parts along dimension 0, may hold values from 0 to 1, as said below
Outputs:
- attended: bfloat16 [2048, 4096], P(('groups', 'section', 'seq')), parts along dimension 0
There are 2 independent parts, one for each index of `groups`. A program takes and returns all parts, laid end to end along the dimension named above; an argument that names none is the same for every part. Nothing has to cross between parts.
Inputs may be any that keep to these rules, and one draw needn't show every extreme that they name: `span_mask`: row a is 1 at column a and 0 at every column after a; the last row is all ones.
All inputs are finite; a program needn't handle non-finite values.
Results may differ from a plain program's by a relative error of at most 0.0038.
The roundings to bfloat16 on the way count: a program that leaves them out, or rounds other values in their place, can miss the bound.
Values may be sent and summed in bfloat16 or wider, within the bound.
A program may use at most 64 MiB of HBM per device.

v0:
```python
import math

import jax
import jax.numpy as jnp
from jax import lax
from jax.sharding import PartitionSpec as P

HEADS = 32
HEAD_DIM = 128


def normalize(rows, gain):
    floats = rows.astype(jnp.float32)
    factor = lax.rsqrt(jnp.mean(floats * floats, axis=-1, keepdims=True) + 1e-06)
    return (floats * factor * gain).astype(jnp.bfloat16)


def body(queries, keys, values, query_gain, key_gain, placement, span_mask):
    tok_rows = queries.shape[0]
    seq_count = lax.axis_size("seq")
    local_heads = HEADS // seq_count
    sections = placement.shape[0]
    span_len = tok_rows * seq_count
    score_scale = 1.0 / HEAD_DIM**0.5
    normed_q = normalize(queries, query_gain).reshape(tok_rows, HEADS, HEAD_DIM)
    normed_k = normalize(keys, key_gain)
    section_ids = jnp.arange(sections, dtype=jnp.int32)
    my_section = lax.axis_index("section")
    my_span = jnp.sum(jnp.where(section_ids == my_section, placement, 0))
    mask_row = jnp.sum(jnp.where((section_ids == my_span)[:, None], span_mask, 0), axis=0)
    section_open = jnp.sum(
        jnp.where(placement[:, None] == section_ids[None, :], mask_row[None, :], 0), axis=1
    )
    initial = (
        jnp.full((local_heads, span_len), -1e30, jnp.float32),
        jnp.zeros((local_heads, span_len), jnp.float32),
        jnp.zeros((span_len, local_heads, HEAD_DIM), jnp.float32),
    )
    window_k, window_v = (
        lax.all_gather(normed_k, "section", axis=0, tiled=True),
        lax.all_gather(values, "section", axis=0, tiled=True),
    )
    window_k = window_k.reshape(sections, tok_rows, HEADS, HEAD_DIM)
    window_v = window_v.reshape(sections, tok_rows, HEADS, HEAD_DIM)
    query_heads = lax.all_to_all(normed_q, "seq", split_axis=1, concat_axis=0, tiled=True)
    heads_k, heads_v = (
        lax.all_to_all(window_k, "seq", split_axis=2, concat_axis=1, tiled=True),
        lax.all_to_all(window_v, "seq", split_axis=2, concat_axis=1, tiled=True),
    )
    heads_k = heads_k.reshape(sections * span_len, local_heads, HEAD_DIM)
    heads_v = heads_v.reshape(sections * span_len, local_heads, HEAD_DIM)
    piece_rows = heads_k.shape[0]
    block_len = math.gcd(piece_rows, 512)
    block_count = piece_rows // block_len
    key_blocks = heads_k.reshape(block_count, block_len, local_heads, HEAD_DIM)
    value_blocks = heads_v.reshape(block_count, block_len, local_heads, HEAD_DIM)
    block_firsts = jnp.arange(block_count, dtype=jnp.int32) * block_len

    def one_block(state_in, block):
        running_max, totals, weighted = state_in
        key_block, value_block, block_first = block
        key_section = (block_first + jnp.arange(block_len, dtype=jnp.int32)) // span_len
        opened = (
            jnp.sum(
                jnp.where(key_section[:, None] == section_ids[None, :], section_open[None, :], 0),
                axis=1,
            )
            > 0
        )
        scores = (
            jnp.einsum("qhd,khd->hqk", query_heads, key_block, preferred_element_type=jnp.float32)
            * score_scale
        )
        scores = jnp.where(opened[None, None, :], scores, -1e30)
        new_max = jnp.maximum(running_max, jnp.max(scores, axis=2))
        weights = jnp.where(
            opened[None, None, :], jnp.exp(scores - new_max[:, :, None]), 0.0
        ).astype(jnp.bfloat16)
        shrink = jnp.exp(running_max - new_max)
        totals = totals * shrink + jnp.sum(weights.astype(jnp.float32), axis=2)
        weighted = weighted * shrink.T[:, :, None] + jnp.einsum(
            "hqk,khd->qhd", weights, value_block, preferred_element_type=jnp.float32
        )
        return ((new_max, totals, weighted), None)

    state_out, unused = lax.scan(one_block, initial, (key_blocks, value_blocks, block_firsts))
    running_max, totals, weighted = state_out
    head_out = (weighted / totals.T[:, :, None]).astype(jnp.bfloat16)
    token_out = lax.all_to_all(head_out, "seq", split_axis=0, concat_axis=1, tiled=True)
    return token_out.reshape(tok_rows, HEADS * HEAD_DIM)


def solution(mesh):
    return jax.shard_map(
        body,
        mesh=mesh,
        in_specs=(
            P(("groups", "section", "seq"), None),
            P(("groups", "section", "seq"), None),
            P(("groups", "section", "seq"), None),
            P(),
            P(),
            P("groups"),
            P("groups", None),
        ),
        out_specs=P(("groups", "section", "seq"), None),
        check_vma=False,
    )
```

profile of v0, /device:TPU:0, one launch (start us, length us, event | category | flops | bytes accessed | tf_op | source)
XLA Modules:
  0.0 180.8 jit_solution(18211372339065865746)
XLA Ops:
  8.6 2.0 %fusion.15 = bf16[64,4096]{1,0:T(8,128)(2,1)} fusion(bf16[64,4096]{1,0:T(8,128)(2,1)} %param.10, f32[4096]{0:T(1024)} %param.13, f32[64]{0:T(128)S(1)} %add_rsqrt_fusion.1), kind=kLoop, calls=%fused_computation.39 | loop fusion | flops 1048576 | bytes 1065216 | tf_op jit(solution)/shard_map/convert_element_type | solution.py:15
  10.6 1.2 fusion.16
  11.9 2.1 %copy_bitcast_fusion.3 = bf16[64,32,128]{2,0,1:T(8,128)(2,1)} fusion(bf16[64,4096]{1,0:T(8,128)(2,1)} %param.9, f32[4096]{0:T(1024)} %param.12, f32[64]{0:T(128)S(1)} %add_rsqrt_fusion), kind=kLoop, calls=%fused_computation.46 | loop fusion | flops 1048576 | bytes 1065216 | tf_op jit(solution)/shard_map/reshape | solution.py:25
  14.0 4.2 %all-to-all-start.1 = ((bf16[64,32,128]{2,0,1:T(8,128)(2,1)}), bf16[64,32,128]{2,0,1:T(8,128)(2,1)S(1)}, u32[]{:S(2)}, u32[]{:S(2)}) async-start(bf16[64,32,128]{2,0,1:T(8,128)(2,1)} %copy_bitcast_fusion.3), calls=%async_computation.1 | async-start | bytes 1048576 | tf_op jit(solution)/shard_map/all_to_all | solution.py:45
  18.2 39.4 %all-gather.5.cloned.1.call-done = bf16[256,4096]{1,0:T(8,128)(2,1)} async-done(((bf16[64,4096]{1,0:T(8,128)(2,1)}), bf16[256,4096]{1,0:T(8,128)(2,1)}) %all-gather.5.cloned.1.call-update) | async-done | bytes 2097168 | tf_op jit(solution)/shard_map/all_gather | solution.py:41
  57.6 2.1 %copy.78 = bf16[32,8,32,128]{3,2,1,0:T(8,128)(2,1)S(1)} copy(bf16[32,8,32,128]{3,1,2,0:T(8,128)(2,1)} %bitcast.81) | data formatting | bytes 4194304
  59.7 2.1 %copy.61 = bf16[4,64,32,128]{3,1,0,2:T(8,128)(2,1)} copy(bf16[4,64,32,128]{3,2,1,0:T(8,128)(2,1)S(1)} %bitcast.78) | data formatting | bytes 4194304 | tf_op jit(solution)/shard_map/reshape | solution.py:44
  61.8 3.6 %all-to-all-start.2 = ((bf16[4,64,32,128]{3,1,0,2:T(8,128)(2,1)}), bf16[4,64,32,128]{3,1,0,2:T(8,128)(2,1)S(1)}, u32[]{:S(2)}, u32[]{:S(2)}) async-start(bf16[4,64,32,128]{3,1,0,2:T(8,128)(2,1)} %copy.61), calls=%async_computation.2 | async-start | bytes 4194304 | tf_op jit(solution)/shard_map/all_to_all | solution.py:48
  65.5 38.4 %all-gather.3.cloned.1.call-done = bf16[256,4096]{1,0:T(8,128)(2,1)} async-done(((bf16[64,4096]{1,0:T(8,128)(2,1)}), bf16[256,4096]{1,0:T(8,128)(2,1)}) %all-gather.3.cloned.1.call-update) | async-done | bytes 2097168 | tf_op jit(solution)/shard_map/all_gather | solution.py:40
  103.9 2.1 %copy.77 = bf16[32,8,32,128]{3,2,1,0:T(8,128)(2,1)S(1)} copy(bf16[32,8,32,128]{3,1,2,0:T(8,128)(2,1)} %bitcast.80) | data formatting | bytes 4194304
  106.0 2.1 %copy.55 = bf16[4,64,32,128]{3,1,0,2:T(8,128)(2,1)} copy(bf16[4,64,32,128]{3,2,1,0:T(8,128)(2,1)S(1)} %bitcast.79) | data formatting | bytes 4194304 | tf_op jit(solution)/shard_map/reshape | solution.py:43
  108.1 4.4 %all-to-all-start = ((bf16[4,64,32,128]{3,1,0,2:T(8,128)(2,1)}), bf16[4,64,32,128]{3,1,0,2:T(8,128)(2,1)}, u32[]{:S(2)}, u32[]{:S(2)}) async-start(bf16[4,64,32,128]{3,1,0,2:T(8,128)(2,1)} %copy.55), calls=%async_computation | async-start | bytes 4194304 | tf_op jit(solution)/shard_map/all_to_all | solution.py:47
  114.2 1.4 copy.60
  116.4 3.2 %copy.63 = bf16[4,4,64,8,128]{4,3,2,1,0:T(8,128)(2,1)} copy(bf16[4,4,64,8,128]{4,2,0,3,1:T(8,128)(2,1)S(1)} %bitcast.77) | data formatting | bytes 4194304 | tf_op jit(solution)/shard_map/all_to_all | solution.py:48
  119.6 18.7 %all-to-all-done = bf16[4,64,32,128]{3,1,0,2:T(8,128)(2,1)} async-done(((bf16[4,64,32,128]{3,1,0,2:T(8,128)(2,1)}), bf16[4,64,32,128]{3,1,0,2:T(8,128)(2,1)}, u32[]{:S(2)}, u32[]{:S(2)}) %all-to-all-start) | async-done | bytes 2097184 | tf_op jit(solution)/shard_map/all_to_all | solution.py:47
  138.3 4.7 %copy.57 = bf16[4,4,64,8,128]{4,3,2,1,0:T(8,128)(2,1)} copy(bf16[4,4,64,8,128]{4,2,0,3,1:T(8,128)(2,1)} %bitcast.2) | data formatting | bytes 4194304 | tf_op jit(solution)/shard_map/all_to_all | solution.py:47
  142.9 17.7 %while.17 = (s32[]{:T(128)}, f32[8,256]{1,0:T(8,128)S(1)}, f32[8,256]{1,0:T(8,128)S(1)}, f32[256,8,128]{0,2,1:T(8,128)S(1)}, s32[2]{0:T(128)S(1)}, /*index=5*/s3...) while((s32[]{:T(128)}, f32[8,256]{1,0:T(8,128)S(1)}, ...), condition=%wide.region_9.10_spmd.clone, body=%wide.region_5.9_spmd.clone.sunk | while | flops 548169728 | bytes 23725732 | solution.py:86
  144.3 2.7 %constant_dynamic-slice_fusion.3 = (bf16[1,512,8,128]{3,2,1,0:T(8,128)(2,1)S(1)}, bf16[1,512,8,128]{3,2,1,0:T(8,128)(2,1)}) fusion(bf16[2,512,8,128]{3,2,1,0:T(8,128)(2,1)} %get-tuple-element.338, s32[]{:T(128)S(6)} %copy.95, bf16[2,512,8,128]{3,2,1,0:T(8,128)(2,1)} %get-tuple-element.336), kind=kLoop, calls=%fused_computation.31.clone.1 | loop fusion | bytes 4194308 | tf_op jit(solution)/shard_map/while/body/jit(dynamic_index_in_dim)/dynamic_slice | solution.py:86
  147.6 2.1 %bitcast_reduce_fusion.2 = (f32[8,256]{1,0:T(8,128)S(1)}, f32[8,512,256]{2,1,0:T(8,128)S(1)}) fusion(pred[512]{0:T(512)(128)(4,1)S(1)} %broadcast_compare_fusion.2, bf16[256,8,128]{2,0,1:T(8,128)(2,1)} %get-tuple-element.337, bf16[1,512,8,128]{3,2,1,0:T(8,128)(2,1)} %get-tuple-element.300), kind=kOutput, calls=%fused_computation.2.clone.1 | convolution fusion | flops 271579136 | bytes 5775872 | tf_op jit(solution)/shard_map/while/body/eval_jaxpr/qhd,khd->hqk/dot_general | solution.py:71
  149.7 1.4 convert_reduce_fusion.2
  153.1 2.7 %constant_dynamic-slice_fusion.3 = (bf16[1,512,8,128]{3,2,1,0:T(8,128)(2,1)S(1)}, bf16[1,512,8,128]{3,2,1,0:T(8,128)(2,1)}) fusion(bf16[2,512,8,128]{3,2,1,0:T(8,128)(2,1)} %get-tuple-element.338, s32[]{:T(128)S(6)} %copy.95, bf16[2,512,8,128]{3,2,1,0:T(8,128)(2,1)} %get-tuple-element.336), kind=kLoop, calls=%fused_computation.31.clone.1 | loop fusion | bytes 4194308 | tf_op jit(solution)/shard_map/while/body/jit(dynamic_index_in_dim)/dynamic_slice | solution.py:86
  156.5 2.1 %bitcast_reduce_fusion.2 = (f32[8,256]{1,0:T(8,128)S(1)}, f32[8,512,256]{2,1,0:T(8,128)S(1)}) fusion(pred[512]{0:T(512)(128)(4,1)S(1)} %broadcast_compare_fusion.2, bf16[256,8,128]{2,0,1:T(8,128)(2,1)} %get-tuple-element.337, bf16[1,512,8,128]{3,2,1,0:T(8,128)(2,1)} %get-tuple-element.300), kind=kOutput, calls=%fused_computation.2.clone.1 | convolution fusion | flops 271579136 | bytes 5775872 | tf_op jit(solution)/shard_map/while/body/eval_jaxpr/qhd,khd->hqk/dot_general | solution.py:71
  158.6 1.4 convert_reduce_fusion.2
  161.6 11.2 %all_to_all.63 = bf16[256,8,128]{2,1,0:T(8,128)(2,1)S(1)} all-to-all(bf16[256,8,128]{2,1,0:T(8,128)(2,1)S(1)} %divide_convert_fusion), channel_id=1, replica_groups=mesh['groups'=2,'section'=4,'seq'=4] {'seq'}, dimensions={0} | all-to-all | bytes 1048576 | tf_op jit(solution)/shard_map/all_to_all | solution.py:89
  (47 shorter events, 11.6 us)
Async XLA Ops:
  6.5 51.1 %all-gather.5.cloned.1.call-start = ((), (), s32[]{:S(2)}) async-start(), calls=%async_computation.5 | async-start | bytes 2621440 | tf_op jit(solution)/shard_map/all_gather | solution.py:41
  7.3 96.6 %all-gather.3.cloned.1.call-start = ((), (), s32[]{:S(2)}) async-start(), calls=%async_computation.4 | async-start | bytes 2621440 | tf_op jit(solution)/shard_map/all_gather | solution.py:40
  14.0 47.8 %all-to-all-start.1 = ((bf16[64,32,128]{2,0,1:T(8,128)(2,1)}), bf16[64,32,128]{2,0,1:T(8,128)(2,1)S(1)}, u32[]{:S(2)}, u32[]{:S(2)}) async-start(bf16[64,32,128]{2,0,1:T(8,128)(2,1)} %copy_bitcast_fusion.3), calls=%async_computation.1 | async-start | bytes 1048576 | tf_op jit(solution)/shard_map/all_to_all | solution.py:45
  61.8 44.1 %copy-start = (bf16[64,32,128]{2,0,1:T(8,128)(2,1)}, bf16[64,32,128]{2,0,1:T(8,128)(2,1)S(1)}, u32[]{:S(2)}) copy-start(bf16[64,32,128]{2,0,1:T(8,128)(2,1)S(1)} %all-to-all-done.1) | copy-start | bytes 1572868
  61.8 46.2 %all-to-all-start.2 = ((bf16[4,64,32,128]{3,1,0,2:T(8,128)(2,1)}), bf16[4,64,32,128]{3,1,0,2:T(8,128)(2,1)S(1)}, u32[]{:S(2)}, u32[]{:S(2)}) async-start(bf16[4,64,32,128]{3,1,0,2:T(8,128)(2,1)} %copy.61), calls=%async_computation.2 | async-start | bytes 4194304 | tf_op jit(solution)/shard_map/all_to_all | solution.py:48
  105.9 6.6 %copy-start.2 = (s32[4]{0:T(128)S(1)}, s32[4]{0:T(128)}, u32[]{:S(2)}) copy-start(s32[4]{0:T(128)} %param.14) | copy-start | bytes 52
  105.9 7.9 %copy-start.1 = (s32[4,4]{1,0:T(4,128)S(1)}, s32[4,4]{1,0:T(4,128)}, u32[]{:S(2)}) copy-start(s32[4,4]{1,0:T(4,128)} %param.15) | copy-start | bytes 196
  108.1 30.2 %all-to-all-start = ((bf16[4,64,32,128]{3,1,0,2:T(8,128)(2,1)}), bf16[4,64,32,128]{3,1,0,2:T(8,128)(2,1)}, u32[]{:S(2)}, u32[]{:S(2)}) async-start(bf16[4,64,32,128]{3,1,0,2:T(8,128)(2,1)} %copy.55), calls=%async_computation | async-start | bytes 4194304 | tf_op jit(solution)/shard_map/all_to_all | solution.py:47
Sparse Core Ops, SparseCore 0:
  8.9 48.6 all-gather.4
  59.2 44.6 all-gather.2
where the time goes:
time: 182 us; the launch traced here: 181 us
  waiting for transfers between devices  97.2 us (53%)
  local copies, waits for them, and re-layouts  27.9 us (15%)
  between operations  13.6 us (7%)
  other arithmetic  12.9 us (7%)
  starting transfers between devices  12.4 us (7%)
  blocking collectives  11.2 us (6%)
  matrix products  5.42 us (3%)
    all_gather x1, waiting for transfers between devices, body(): lax.all_gather(values, 'section', axis=0, tiled=True)  39.4 us
    all_gather x1, waiting for transfers between devices, body(): lax.all_gather(normed_k, 'section', axis=0, tiled=True)  38.4 us
    all_to_all x1, waiting for transfers between devices, body(): lax.all_to_all(window_k, 'seq', split_axis=2, concat_axis=1, tiled=True)  18.7 us
    all_to_all x1, blocking collectives, body(): lax.all_to_all(head_out, 'seq', split_axis=0, concat_axis=1, tiled=True)  11.2 us
    dynamic_slice x6, local copies, waits for them, and re-layouts, body(): lax.scan(one_block, initial, (key_blocks, value_blocks, block_firsts))  7.82 us
    unnamed x10, local copies, waits for them, and re-layouts  6.03 us
    all_to_all x1, local copies, waits for them, and re-layouts, body(): lax.all_to_all(window_k, 'seq', split_axis=2, concat_axis=1, tiled=True)  4.65 us
    all_to_all x1, starting transfers between devices, body(): lax.all_to_all(window_k, 'seq', split_axis=2, concat_axis=1, tiled=True)  4.44 us
  transfers between devices with their start and end apart: 5, of which 3 were waited for; matrix products, arithmetic and copies ran while one was open for 12% of the time, Pallas kernels for 0%

commit v1 on v0

--- a/solution.py
+++ b/solution.py
@@ -1,12 +1,249 @@
+import functools
 import math
 
 import jax
 import jax.numpy as jnp
 from jax import lax
+from jax.experimental import pallas as pl
+from jax.experimental.pallas import tpu as pltpu
 from jax.sharding import PartitionSpec as P
 
 HEADS = 32
 HEAD_DIM = 128
+MESH = pl.DeviceIdType.MESH
+
+
+def flipped(index, flips, count):
+    result = index
+    bit = 1
+    while bit < count:
+        result = result + ((flips // bit) % 2) * bit * (1 - 2 * ((index // bit) % 2))
+        bit *= 2
+    return result
+
+
+def kernel(
+    sections,
+    seq_count,
+    q_ref,
+    k_ref,
+    v_ref,
+    query_gain,
+    key_gain,
+    placement,
+    span_mask,
+    out_ref,
+    norm_q,
+    norm_k,
+    all_q,
+    all_k,
+    all_v,
+    result,
+    in_send,
+    in_recv,
+    out_send,
+    out_recv,
+    own_sem,
+):
+    rows = q_ref.shape[0]
+    count = sections * seq_count
+    own_heads = HEADS // count
+    span_len = rows * seq_count
+    section = lax.axis_index("section")
+    seq = lax.axis_index("seq")
+    me = section * seq_count + seq
+    first_row = pl.multiple_of(me * rows, rows)
+
+    def peer(step):
+        to_section = flipped(section, step // seq_count, sections)
+        to_seq = flipped(seq, step % seq_count, seq_count)
+        return to_section, to_seq
+
+    def start_of(device, head):
+        return pl.multiple_of((device * own_heads + head) * HEAD_DIM, HEAD_DIM)
+
+    barrier = pltpu.get_barrier_semaphore()
+
+    def greet(step, carry):
+        to_section, to_seq = peer(step)
+        pl.semaphore_signal(
+            barrier, inc=1, device_id={"section": to_section, "seq": to_seq}, device_id_type=MESH
+        )
+        return carry
+
+    lax.fori_loop(1, count, greet, 0)
+    all_v[:, :, HEAD_DIM:] = jnp.ones((own_heads, count * rows, HEAD_DIM), jnp.bfloat16)
+
+    def normalize(source, gain, target):
+        def chunk(index, carry):
+            part = pl.ds(pl.multiple_of(index * 16, 16), 16)
+            floats = source[part, :].astype(jnp.float32)
+            factor = lax.rsqrt(jnp.mean(floats * floats, axis=-1, keepdims=True) + 1e-06)
+            target[part, :] = (floats * factor * gain[...]).astype(jnp.bfloat16)
+            return carry
+
+        lax.fori_loop(0, rows // 16, chunk, 0)
+
+    def incoming(which, source, target, head, step):
+        to_section, to_seq = peer(step)
+        device = to_section * seq_count + to_seq
+        return pltpu.make_async_remote_copy(
+            src_ref=source.at[:, pl.ds(start_of(device, head), HEAD_DIM)],
+            dst_ref=target.at[head, pl.ds(first_row, rows), pl.ds(0, HEAD_DIM)],
+            send_sem=in_send.at[which, head, step],
+            recv_sem=in_recv.at[which, head, step],
+            device_id={"section": to_section, "seq": to_seq},
+            device_id_type=MESH,
+        )
+
+    def send(which, source, target, head):
+        def one(index, carry):
+            incoming(which, source, target, head, count - 1 - index).start()
+            return carry
+
+        lax.fori_loop(0, count - 1, one, 0)
+        target[head, pl.ds(first_row, rows), pl.ds(0, HEAD_DIM)] = source[
+            :, pl.ds(start_of(me, head), HEAD_DIM)
+        ]
+
+    triples = ((0, v_ref, all_v), (1, norm_k, all_k), (2, norm_q, all_q))
+    normalize(k_ref, key_gain, norm_k)
+    pl.semaphore_wait(barrier, count - 1)
+    send(*triples[0], 0)
+    send(*triples[1], 0)
+    normalize(q_ref, query_gain, norm_q)
+    send(*triples[2], 0)
+    for head in range(1, own_heads):
+        for triple in triples:
+            send(*triple, head)
+
+    def outgoing(head, step):
+        to_section, to_seq = peer(step)
+        source_row = pl.multiple_of((to_section * seq_count + to_seq) * rows, rows)
+        return pltpu.make_async_remote_copy(
+            src_ref=result.at[head, pl.ds(source_row, rows), :],
+            dst_ref=out_ref.at[:, pl.ds(start_of(me, head), HEAD_DIM)],
+            send_sem=out_send.at[head, step],
+            recv_sem=out_recv.at[head, step],
+            device_id={"section": to_section, "seq": to_seq},
+            device_id_type=MESH,
+        )
+
+    def kept(head):
+        return pltpu.make_async_copy(
+            result.at[head, pl.ds(first_row, rows), :],
+            out_ref.at[:, pl.ds(start_of(me, head), HEAD_DIM)],
+            own_sem.at[head],
+        )
+
+    factor = 1.0 / HEAD_DIM**0.5 * math.log2(math.e)
+
+    def attend(head, flips):
+        row_section = flipped(section, flips, sections)
+        row = pl.multiple_of(row_section * span_len, span_len)
+        query = all_q[head, pl.ds(row, span_len), :]
+        row_span = placement[row_section]
+        scores, shut = [], []
+        top = None
+        for key_section in range(sections):
+            key = all_k[head, key_section * span_len : (key_section + 1) * span_len, :]
+            block = lax.dot_general(
+                query, key, (((1,), (1,)), ((), ())), preferred_element_type=jnp.float32
+            )
+            opened = span_mask[row_span, placement[key_section]]
+            closed = (opened - 1).astype(jnp.float32) * 1e30
+            block_top = jnp.max(block, axis=1, keepdims=True) + closed
+            top = block_top if top is None else jnp.maximum(top, block_top)
+            scores.append(block)
+            shut.append(closed)
+        total = jnp.zeros((span_len, 2 * HEAD_DIM), jnp.float32)
+        for key_section in range(sections):
+            offset = top * factor - shut[key_section]
+            weights = jnp.exp2(scores[key_section] * factor - offset).astype(jnp.bfloat16)
+            value = all_v[head, key_section * span_len : (key_section + 1) * span_len, :]
+            total = total + jnp.dot(weights, value, preferred_element_type=jnp.float32)
+        result[head, pl.ds(row, span_len), :] = (
+            total[:, :HEAD_DIM] / total[:, HEAD_DIM:]
+        ).astype(jnp.bfloat16)
+
+    for head in range(own_heads):
+
+        def arrived(step, carry):
+            for triple in triples:
+                incoming(*triple, head, step).wait_recv()
+            return carry
+
+        lax.fori_loop(1, count, arrived, 0)
+
+        def tile(index, carry):
+            flips = sections - 1 - index
+            attend(head, flips)
+
+            def give(other, inner):
+                step = flips * seq_count + other
+
+                @pl.when(step > 0)
+                def _():
+                    outgoing(head, step).start()
+
+                return inner
+
+            lax.fori_loop(0, seq_count, give, 0)
+            return carry
+
+        lax.fori_loop(0, sections, tile, 0)
+        kept(head).start()
+
+    def drain(step, carry):
+        for head in range(own_heads):
+            for triple in triples:
+                incoming(*triple, head, step).wait_send()
+            outgoing(head, step).wait()
+        return carry
+
+    lax.fori_loop(1, count, drain, 0)
+    for head in range(own_heads):
+        kept(head).wait()
+
+
+def spread(queries, keys, values, query_gain, key_gain, placement, span_mask):
+    rows, width = queries.shape
+    sections, seq_count = lax.axis_size("section"), lax.axis_size("seq")
+    count = sections * seq_count
+    own_heads = HEADS // count
+    tokens = count * rows
+    vmem = pl.BlockSpec(memory_space=pltpu.VMEM)
+    smem = pl.BlockSpec(memory_space=pltpu.SMEM)
+    return pl.pallas_call(
+        functools.partial(kernel, sections, seq_count),
+        out_shape=jax.ShapeDtypeStruct((rows, width), jnp.bfloat16),
+        in_specs=[vmem, vmem, vmem, vmem, vmem, smem, smem],
+        out_specs=pl.BlockSpec(memory_space=pl.ANY),
+        scratch_shapes=[
+            pltpu.VMEM((rows, width), jnp.bfloat16),
+            pltpu.VMEM((rows, width), jnp.bfloat16),
+            pltpu.VMEM((own_heads, tokens, HEAD_DIM), jnp.bfloat16),
+            pltpu.VMEM((own_heads, tokens, HEAD_DIM), jnp.bfloat16),
+            pltpu.VMEM((own_heads, tokens, 2 * HEAD_DIM), jnp.bfloat16),
+            pltpu.VMEM((own_heads, tokens, HEAD_DIM), jnp.bfloat16),
+            pltpu.SemaphoreType.DMA((3, own_heads, count)),
+            pltpu.SemaphoreType.DMA((3, own_heads, count)),
+            pltpu.SemaphoreType.DMA((own_heads, count)),
+            pltpu.SemaphoreType.DMA((own_heads, count)),
+            pltpu.SemaphoreType.DMA((own_heads,)),
+        ],
+        compiler_params=pltpu.CompilerParams(
+            collective_id=0, has_side_effects=True, vmem_limit_bytes=40 * 1024 * 1024
+        ),
+    )(
+        queries,
+        keys,
+        values,
+        query_gain.reshape(1, width),
+        key_gain.reshape(1, width),
+        placement,
+        span_mask,
+    )
 
 
 def normalize(rows, gain):
@@ -91,8 +328,10 @@
 
 
 def solution(mesh):
+    devices = mesh.shape["section"] * mesh.shape["seq"]
+    even = HEADS % devices == 0 and devices & (devices - 1) == 0
     return jax.shard_map(
-        body,
+        spread if even else body,
         mesh=mesh,
         in_specs=(
             P(("groups", "section", "seq"), None),

time: 182 us -> 61.6 us (0.34)
  waiting for transfers between devices: 97.2 us -> 0 us
  Pallas kernels: 0 us -> 55.2 us
  local copies, waits for them, and re-layouts: 27.9 us -> 6.04 us
  between operations: 13.6 us -> 0.02 us
  other arithmetic: 12.9 us -> 0 us
  starting transfers between devices: 12.4 us -> 0 us
  blocking collectives: 11.2 us -> 0 us
  matrix products: 5.42 us -> 0 us
    all_gather x2 -> x0, waiting for transfers between devices: 77.8 us -> none  [the longest x1 39.4 us: body(): lax.all_gather(values, 'section', axis=0, tiled=True)]
    pallas_call x0 -> x1, Pallas kernels: none -> 55.2 us  [spread(): pl.pallas_call(functools.partial(kernel, sections, seq_count), out_shape=...]
    all_to_all x3 -> x0, waiting for transfers between devices: 18.7 us -> none  [the longest x1 18.7 us: body(): lax.all_to_all(window_k, 'seq', split_axis=2, concat_axis=1, tiled=True)]
    all_to_all x3 -> x0, starting transfers between devices: 12.3 us -> none  [the longest x1 4.44 us: body(): lax.all_to_all(window_k, 'seq', split_axis=2, concat_axis=1, tiled=True)]
    all_to_all x1 -> x0, blocking collectives: 11.2 us -> none  [body(): lax.all_to_all(head_out, 'seq', split_axis=0, concat_axis=1, tiled=True)]
    all_to_all x4 -> x0, local copies, waits for them, and re-layouts: 9.28 us -> none  [the longest x1 4.65 us: body(): lax.all_to_all(window_k, 'seq', split_axis=2, concat_axis=1, tiled=True)]
    dynamic_slice x6 -> x0, local copies, waits for them, and re-layouts: 7.82 us -> none  [body(): lax.scan(one_block, initial, (key_blocks, value_blocks, block_firsts))]
    reduce_sum x9 -> x0, other arithmetic: 6.44 us -> none  [the longest x2 2.88 us: one_block(): totals = totals * shrink + jnp.sum(weights.astype(jnp.float32), axis=2)]
  transfers between devices with their start and end apart: 5 -> 0, of which waited for: 3 -> 0; matrix products, arithmetic and copies ran while one was open for 12% -> 0% of each run, Pallas kernels for 0% -> 0%
where the time goes in v1:
time: 61.6 us; the launch traced here: 61.3 us
  Pallas kernels  55.2 us (90%)
  local copies, waits for them, and re-layouts  6.04 us (10%)
    pallas_call x1, Pallas kernels, spread(): pl.pallas_call(functools.partial(kernel, sections, seq_count), out_shape=...  55.2 us
    unnamed x15, local copies, waits for them, and re-layouts  6.04 us

profile of v1, /device:TPU:0, one launch (start us, length us, event | category | flops | bytes accessed | tf_op | source)
XLA Modules:
  0.0 61.3 jit_solution(11481662002759354921)
XLA Ops:
  0.0 0.0 copy-start.5
  0.0 0.0 copy-start.6
  0.0 0.7 %copy-done.5 = s32[4,4]{1,0:T(4,128)S(1)} copy-done((s32[4,4]{1,0:T(4,128)S(1)}, s32[4,4]{1,0:T(4,128)}, u32[]{:S(2)}) %copy-start.5) | copy-done | bytes 88
  0.7 0.0 copy-done.6
  0.7 0.0 copy-start
  0.7 1.0 %copy-done = bf16[64,4096]{1,0:T(8,128)(2,1)S(1)} copy-done((bf16[64,4096]{1,0:T(8,128)(2,1)S(1)}, bf16[64,4096]{1,0:T(8,128)(2,1)}, u32[]{:S(2)}) %copy-start) | copy-done | bytes 524312
  1.7 0.0 copy-start.1
  1.7 1.0 %copy-done.1 = bf16[64,4096]{1,0:T(8,128)(2,1)S(1)} copy-done((bf16[64,4096]{1,0:T(8,128)(2,1)S(1)}, bf16[64,4096]{1,0:T(8,128)(2,1)}, u32[]{:S(2)}) %copy-start.1) | copy-done | bytes 524312
  2.8 0.0 copy-start.2
  2.8 1.0 %copy-done.2 = bf16[64,4096]{1,0:T(8,128)(2,1)S(1)} copy-done((bf16[64,4096]{1,0:T(8,128)(2,1)S(1)}, bf16[64,4096]{1,0:T(8,128)(2,1)}, u32[]{:S(2)}) %copy-start.2) | copy-done | bytes 524312
  3.8 0.0 copy-start.3
  3.8 0.7 %copy-done.3 = f32[4096]{0:T(1024)S(1)} copy-done((f32[4096]{0:T(1024)S(1)}, f32[4096]{0:T(1024)}, u32[]{:S(2)}) %copy-start.3) | copy-done | bytes 16408
  4.5 0.0 copy-start.4
  4.5 0.7 %copy-done.4 = f32[4096]{0:T(1024)S(1)} copy-done((f32[4096]{0:T(1024)S(1)}, f32[4096]{0:T(1024)}, u32[]{:S(2)}) %copy-start.4) | copy-done | bytes 16408
  5.2 55.2 %shard_map.73 = bf16[64,4096]{1,0:T(8,128)(2,1)S(1)} custom-call(bf16[64,4096]{1,0:T(8,128)(2,1)S(1)} %copy-done, bf16[64,4096]{1,0:T(8,128)(2,1)S(1)} %copy-done.1, bf16[64,4096]{1,0:T(8,128)(2,1)S(1)} %copy-done.2, f32[1,4096]{1,0:T(1,128)S(1)} %bitcast.2, f32[1,4096]{1,0:T(1,128)S(1)} %bitcast.3, s32[4]{0:T(128)S(1)} %copy-done.6, s32[4,4]{1,0:T(4,128)S(1)} %copy-done.5), custom_call_target="tpu_custom_call" | custom-call | tf_op jit(solution)/shard_map/pallas_call | solution.py:217
  60.5 0.8 %copy.9 = bf16[64,4096]{1,0:T(8,128)(2,1)} copy(bf16[64,4096]{1,0:T(8,128)(2,1)S(1)} %shard_map.73) | data formatting | bytes 1048576
Async XLA Ops:
  0.0 0.7 %copy-start.5 = (s32[4,4]{1,0:T(4,128)S(1)}, s32[4,4]{1,0:T(4,128)}, u32[]{:S(2)}) copy-start(s32[4,4]{1,0:T(4,128)} %span_mask.1) | copy-start | bytes 196
  0.0 0.7 %copy-start.6 = (s32[4]{0:T(128)S(1)}, s32[4]{0:T(128)}, u32[]{:S(2)}) copy-start(s32[4]{0:T(128)} %placement.1) | copy-start | bytes 52
  0.7 1.0 %copy-start = (bf16[64,4096]{1,0:T(8,128)(2,1)S(1)}, bf16[64,4096]{1,0:T(8,128)(2,1)}, u32[]{:S(2)}) copy-start(bf16[64,4096]{1,0:T(8,128)(2,1)} %q_ref.1) | copy-start | bytes 1572868
  1.7 1.0 %copy-start.1 = (bf16[64,4096]{1,0:T(8,128)(2,1)S(1)}, bf16[64,4096]{1,0:T(8,128)(2,1)}, u32[]{:S(2)}) copy-start(bf16[64,4096]{1,0:T(8,128)(2,1)} %k_ref.1) | copy-start | bytes 1572868
  2.8 1.0 %copy-start.2 = (bf16[64,4096]{1,0:T(8,128)(2,1)S(1)}, bf16[64,4096]{1,0:T(8,128)(2,1)}, u32[]{:S(2)}) copy-start(bf16[64,4096]{1,0:T(8,128)(2,1)} %v_ref.1) | copy-start | bytes 1572868
  3.8 0.7 %copy-start.3 = (f32[4096]{0:T(1024)S(1)}, f32[4096]{0:T(1024)}, u32[]{:S(2)}) copy-start(f32[4096]{0:T(1024)} %param.10) | copy-start | bytes 49156
  4.5 0.7 %copy-start.4 = (f32[4096]{0:T(1024)S(1)}, f32[4096]{0:T(1024)}, u32[]{:S(2)}) copy-start(f32[4096]{0:T(1024)} %param.11) | copy-start | bytes 49156

commit v2 on v1

--- a/solution.py
+++ b/solution.py
@@ -59,8 +59,9 @@
         to_seq = flipped(seq, step % seq_count, seq_count)
         return to_section, to_seq
 
-    def start_of(device, head):
-        return pl.multiple_of((device * own_heads + head) * HEAD_DIM, HEAD_DIM)
+    def columns_of(device):
+        width = own_heads * HEAD_DIM
+        return pl.ds(pl.multiple_of(device * width, width), width)
 
     barrier = pltpu.get_barrier_semaphore()
 
@@ -72,7 +73,6 @@
         return carry
 
     lax.fori_loop(1, count, greet, 0)
-    all_v[:, :, HEAD_DIM:] = jnp.ones((own_heads, count * rows, HEAD_DIM), jnp.bfloat16)
 
     def normalize(source, gain, target):
         def chunk(index, carry):
@@ -84,69 +84,61 @@
 
         lax.fori_loop(0, rows // 16, chunk, 0)
 
-    def incoming(which, source, target, head, step):
+    def incoming(which, source, target, step):
         to_section, to_seq = peer(step)
-        device = to_section * seq_count + to_seq
         return pltpu.make_async_remote_copy(
-            src_ref=source.at[:, pl.ds(start_of(device, head), HEAD_DIM)],
-            dst_ref=target.at[head, pl.ds(first_row, rows), pl.ds(0, HEAD_DIM)],
-            send_sem=in_send.at[which, head, step],
-            recv_sem=in_recv.at[which, head, step],
+            src_ref=source.at[:, columns_of(to_section * seq_count + to_seq)],
+            dst_ref=target.at[pl.ds(first_row, rows), :],
+            send_sem=in_send.at[which, step],
+            recv_sem=in_recv.at[which, step],
             device_id={"section": to_section, "seq": to_seq},
             device_id_type=MESH,
         )
 
-    def send(which, source, target, head):
+    def send(which, source, target):
         def one(index, carry):
-            incoming(which, source, target, head, count - 1 - index).start()
+            incoming(which, source, target, count - 1 - index).start()
             return carry
 
         lax.fori_loop(0, count - 1, one, 0)
-        target[head, pl.ds(first_row, rows), pl.ds(0, HEAD_DIM)] = source[
-            :, pl.ds(start_of(me, head), HEAD_DIM)
-        ]
+        target[pl.ds(first_row, rows), :] = source[:, columns_of(me)]
 
     triples = ((0, v_ref, all_v), (1, norm_k, all_k), (2, norm_q, all_q))
     normalize(k_ref, key_gain, norm_k)
     pl.semaphore_wait(barrier, count - 1)
-    send(*triples[0], 0)
-    send(*triples[1], 0)
+    send(*triples[0])
+    send(*triples[1])
     normalize(q_ref, query_gain, norm_q)
-    send(*triples[2], 0)
-    for head in range(1, own_heads):
-        for triple in triples:
-            send(*triple, head)
-
-    def outgoing(head, step):
+    send(*triples[2])
+
+    def outgoing(step):
         to_section, to_seq = peer(step)
         source_row = pl.multiple_of((to_section * seq_count + to_seq) * rows, rows)
         return pltpu.make_async_remote_copy(
-            src_ref=result.at[head, pl.ds(source_row, rows), :],
-            dst_ref=out_ref.at[:, pl.ds(start_of(me, head), HEAD_DIM)],
-            send_sem=out_send.at[head, step],
-            recv_sem=out_recv.at[head, step],
+            src_ref=result.at[pl.ds(source_row, rows), :],
+            dst_ref=out_ref.at[:, columns_of(me)],
+            send_sem=out_send.at[step],
+            recv_sem=out_recv.at[step],
             device_id={"section": to_section, "seq": to_seq},
             device_id_type=MESH,
         )
 
-    def kept(head):
-        return pltpu.make_async_copy(
-            result.at[head, pl.ds(first_row, rows), :],
-            out_ref.at[:, pl.ds(start_of(me, head), HEAD_DIM)],
-            own_sem.at[head],
-        )
+    kept = pltpu.make_async_copy(
+        result.at[pl.ds(first_row, rows), :], out_ref.at[:, columns_of(me)], own_sem
+    )
 
     factor = 1.0 / HEAD_DIM**0.5 * math.log2(math.e)
 
     def attend(head, flips):
+        lanes = slice(head * HEAD_DIM, (head + 1) * HEAD_DIM)
         row_section = flipped(section, flips, sections)
         row = pl.multiple_of(row_section * span_len, span_len)
-        query = all_q[head, pl.ds(row, span_len), :]
+        query = all_q[pl.ds(row, span_len), lanes]
         row_span = placement[row_section]
         scores, shut = [], []
         top = None
         for key_section in range(sections):
-            key = all_k[head, key_section * span_len : (key_section + 1) * span_len, :]
+            key = all_k[key_section * span_len : (key_section + 1) * span_len, lanes]
             block = lax.dot_general(
                 query, key, (((1,), (1,)), ((), ())), preferred_element_type=jnp.float32
             )
@@ -160,50 +152,59 @@
         for key_section in range(sections):
             offset = top * factor - shut[key_section]
             weights = jnp.exp2(scores[key_section] * factor - offset).astype(jnp.bfloat16)
-            value = all_v[head, key_section * span_len : (key_section + 1) * span_len, :]
+            value = all_v[key_section * span_len : (key_section + 1) * span_len, lanes]
+            value = jnp.concatenate([value, jnp.ones_like(value)], axis=1)
             total = total + jnp.dot(weights, value, preferred_element_type=jnp.float32)
-        result[head, pl.ds(row, span_len), :] = (
+        result[pl.ds(row, span_len), lanes] = (
             total[:, :HEAD_DIM] / total[:, HEAD_DIM:]
         ).astype(jnp.bfloat16)
 
-    for head in range(own_heads):
-
-        def arrived(step, carry):
-            for triple in triples:
-                incoming(*triple, head, step).wait_recv()
-            return carry
-
-        lax.fori_loop(1, count, arrived, 0)
-
-        def tile(index, carry):
-            flips = sections - 1 - index
+    def arrived(step, carry):
+        incoming(*triples[0], step).wait_recv()
+        incoming(*triples[1], step).wait_recv()
+        return carry
+
+    lax.fori_loop(1, count, arrived, 0)
+
+    def tile(index, carry):
+        flips = sections - 1 - index
+
+        def take(other, inner):
+            step = flips * seq_count + other
+
+            @pl.when(step > 0)
+            def _():
+                incoming(*triples[2], step).wait_recv()
+
+            return inner
+
+        lax.fori_loop(0, seq_count, take, 0)
+        for head in range(own_heads):
             attend(head, flips)
 
-            def give(other, inner):
-                step = flips * seq_count + other
-
-                @pl.when(step > 0)
-                def _():
-                    outgoing(head, step).start()
-
-                return inner
-
-            lax.fori_loop(0, seq_count, give, 0)
-            return carry
-
-        lax.fori_loop(0, sections, tile, 0)
-        kept(head).start()
+        def give(other, inner):
+            step = flips * seq_count + other
+
+            @pl.when(step > 0)
+            def _():
+                outgoing(step).start()
+
+            return inner
+
+        lax.fori_loop(0, seq_count, give, 0)
+        return carry
+
+    lax.fori_loop(0, sections, tile, 0)
+    kept.start()
 
     def drain(step, carry):
-        for head in range(own_heads):
-            for triple in triples:
-                incoming(*triple, head, step).wait_send()
-            outgoing(head, step).wait()
+        for triple in triples:
+            incoming(*triple, step).wait_send()
+        outgoing(step).wait()
         return carry
 
     lax.fori_loop(1, count, drain, 0)
-    for head in range(own_heads):
-        kept(head).wait()
+    kept.wait()
 
 
 def spread(queries, keys, values, query_gain, key_gain, placement, span_mask):
@@ -222,15 +223,15 @@
         scratch_shapes=[
             pltpu.VMEM((rows, width), jnp.bfloat16),
             pltpu.VMEM((rows, width), jnp.bfloat16),
-            pltpu.VMEM((own_heads, tokens, HEAD_DIM), jnp.bfloat16),
-            pltpu.VMEM((own_heads, tokens, HEAD_DIM), jnp.bfloat16),
-            pltpu.VMEM((own_heads, tokens, 2 * HEAD_DIM), jnp.bfloat16),
-            pltpu.VMEM((own_heads, tokens, HEAD_DIM), jnp.bfloat16),
-            pltpu.SemaphoreType.DMA((3, own_heads, count)),
-            pltpu.SemaphoreType.DMA((3, own_heads, count)),
-            pltpu.SemaphoreType.DMA((own_heads, count)),
-            pltpu.SemaphoreType.DMA((own_heads, count)),
-            pltpu.SemaphoreType.DMA((own_heads,)),
+            pltpu.VMEM((tokens, own_heads * HEAD_DIM), jnp.bfloat16),
+            pltpu.VMEM((tokens, own_heads * HEAD_DIM), jnp.bfloat16),
+            pltpu.VMEM((tokens, own_heads * HEAD_DIM), jnp.bfloat16),
+            pltpu.VMEM((tokens, own_heads * HEAD_DIM), jnp.bfloat16),
+            pltpu.SemaphoreType.DMA((3, count)),
+            pltpu.SemaphoreType.DMA((3, count)),
+            pltpu.SemaphoreType.DMA((count,)),
+            pltpu.SemaphoreType.DMA((count,)),
+            pltpu.SemaphoreType.DMA,
         ],
         compiler_params=pltpu.CompilerParams(
             collective_id=0, has_side_effects=True, vmem_limit_bytes=40 * 1024 * 1024

time: 61.6 us -> 60.2 us (0.977)
  Pallas kernels: 55.2 us -> 53.7 us
    pallas_call x1, Pallas kernels: 55.2 us -> 53.7 us  [spread(): pl.pallas_call(functools.partial(kernel, sections, seq_count), out_shape=...]
where the time goes in v2:
time: 60.2 us; the launch traced here: 59.8 us
  Pallas kernels  53.7 us (89%)
  local copies, waits for them, and re-layouts  6.04 us (10%)
    pallas_call x1, Pallas kernels, spread(): pl.pallas_call(functools.partial(kernel, sections, seq_count), out_shape=...  53.7 us
    unnamed x15, local copies, waits for them, and re-layouts  6.04 us

profile of v2, /device:TPU:0, one launch (start us, length us, event | category | flops | bytes accessed | tf_op | source)
XLA Modules:
  0.0 59.8 jit_solution(1328104217043860456)
XLA Ops:
  0.0 0.0 copy-start.5
  0.0 0.0 copy-start.6
  0.0 0.7 %copy-done.5 = s32[4,4]{1,0:T(4,128)S(1)} copy-done((s32[4,4]{1,0:T(4,128)S(1)}, s32[4,4]{1,0:T(4,128)}, u32[]{:S(2)}) %copy-start.5) | copy-done | bytes 88
  0.7 0.0 copy-done.6
  0.7 0.0 copy-start
  0.7 1.0 %copy-done = bf16[64,4096]{1,0:T(8,128)(2,1)S(1)} copy-done((bf16[64,4096]{1,0:T(8,128)(2,1)S(1)}, bf16[64,4096]{1,0:T(8,128)(2,1)}, u32[]{:S(2)}) %copy-start) | copy-done | bytes 524312
  1.7 0.0 copy-start.1
  1.7 1.0 %copy-done.1 = bf16[64,4096]{1,0:T(8,128)(2,1)S(1)} copy-done((bf16[64,4096]{1,0:T(8,128)(2,1)S(1)}, bf16[64,4096]{1,0:T(8,128)(2,1)}, u32[]{:S(2)}) %copy-start.1) | copy-done | bytes 524312
  2.8 0.0 copy-start.2
  2.8 1.0 %copy-done.2 = bf16[64,4096]{1,0:T(8,128)(2,1)S(1)} copy-done((bf16[64,4096]{1,0:T(8,128)(2,1)S(1)}, bf16[64,4096]{1,0:T(8,128)(2,1)}, u32[]{:S(2)}) %copy-start.2) | copy-done | bytes 524312
  3.8 0.0 copy-start.3
  3.8 0.7 %copy-done.3 = f32[4096]{0:T(1024)S(1)} copy-done((f32[4096]{0:T(1024)S(1)}, f32[4096]{0:T(1024)}, u32[]{:S(2)}) %copy-start.3) | copy-done | bytes 16408
  4.5 0.0 copy-start.4
  4.5 0.7 %copy-done.4 = f32[4096]{0:T(1024)S(1)} copy-done((f32[4096]{0:T(1024)S(1)}, f32[4096]{0:T(1024)}, u32[]{:S(2)}) %copy-start.4) | copy-done | bytes 16408
  5.2 53.7 %shard_map.73 = bf16[64,4096]{1,0:T(8,128)(2,1)S(1)} custom-call(bf16[64,4096]{1,0:T(8,128)(2,1)S(1)} %copy-done, bf16[64,4096]{1,0:T(8,128)(2,1)S(1)} %copy-done.1, bf16[64,4096]{1,0:T(8,128)(2,1)S(1)} %copy-done.2, f32[1,4096]{1,0:T(1,128)S(1)} %bitcast.2, f32[1,4096]{1,0:T(1,128)S(1)} %bitcast.3, s32[4]{0:T(128)S(1)} %copy-done.6, s32[4,4]{1,0:T(4,128)S(1)} %copy-done.5), custom_call_target="tpu_custom_call" | custom-call | tf_op jit(solution)/shard_map/pallas_call | solution.py:218
  59.0 0.8 %copy.9 = bf16[64,4096]{1,0:T(8,128)(2,1)} copy(bf16[64,4096]{1,0:T(8,128)(2,1)S(1)} %shard_map.73) | data formatting | bytes 1048576
Async XLA Ops:
  0.0 0.7 %copy-start.5 = (s32[4,4]{1,0:T(4,128)S(1)}, s32[4,4]{1,0:T(4,128)}, u32[]{:S(2)}) copy-start(s32[4,4]{1,0:T(4,128)} %span_mask.1) | copy-start | bytes 196
  0.0 0.7 %copy-start.6 = (s32[4]{0:T(128)S(1)}, s32[4]{0:T(128)}, u32[]{:S(2)}) copy-start(s32[4]{0:T(128)} %placement.1) | copy-start | bytes 52
  0.7 1.0 %copy-start = (bf16[64,4096]{1,0:T(8,128)(2,1)S(1)}, bf16[64,4096]{1,0:T(8,128)(2,1)}, u32[]{:S(2)}) copy-start(bf16[64,4096]{1,0:T(8,128)(2,1)} %q_ref.1) | copy-start | bytes 1572868
  1.7 1.0 %copy-start.1 = (bf16[64,4096]{1,0:T(8,128)(2,1)S(1)}, bf16[64,4096]{1,0:T(8,128)(2,1)}, u32[]{:S(2)}) copy-start(bf16[64,4096]{1,0:T(8,128)(2,1)} %k_ref.1) | copy-start | bytes 1572868
  2.8 1.0 %copy-start.2 = (bf16[64,4096]{1,0:T(8,128)(2,1)S(1)}, bf16[64,4096]{1,0:T(8,128)(2,1)}, u32[]{:S(2)}) copy-start(bf16[64,4096]{1,0:T(8,128)(2,1)} %v_ref.1) | copy-start | bytes 1572868
  3.8 0.7 %copy-start.3 = (f32[4096]{0:T(1024)S(1)}, f32[4096]{0:T(1024)}, u32[]{:S(2)}) copy-start(f32[4096]{0:T(1024)} %param.10) | copy-start | bytes 49156
  4.5 0.7 %copy-start.4 = (f32[4096]{0:T(1024)S(1)}, f32[4096]{0:T(1024)}, u32[]{:S(2)}) copy-start(f32[4096]{0:T(1024)} %param.11) | copy-start | bytes 49156

commit v3 on v2

--- a/solution.py
+++ b/solution.py
@@ -25,14 +25,20 @@
 def kernel(
     sections,
     seq_count,
+    q_hbm,
+    k_hbm,
+    v_ref,
+    query_gain_hbm,
+    key_gain_hbm,
+    placement_hbm,
+    span_mask_hbm,
+    out_ref,
     q_ref,
     k_ref,
-    v_ref,
     query_gain,
     key_gain,
     placement,
     span_mask,
-    out_ref,
     norm_q,
     norm_k,
     all_q,
@@ -44,6 +50,7 @@
     out_send,
     out_recv,
     own_sem,
+    load_sem,
 ):
     rows = q_ref.shape[0]
     count = sections * seq_count
@@ -63,6 +70,20 @@
         width = own_heads * HEAD_DIM
         return pl.ds(pl.multiple_of(device * width, width), width)
 
+    loads = [
+        pltpu.make_async_copy(source, target, load_sem.at[index])
+        for index, (source, target) in enumerate(
+            (
+                (k_hbm, k_ref),
+                (key_gain_hbm, key_gain),
+                (q_hbm, q_ref),
+                (query_gain_hbm, query_gain),
+                (placement_hbm, placement),
+                (span_mask_hbm, span_mask),
+                (v_ref.at[:, columns_of(me)], all_v.at[pl.ds(first_row, rows), :]),
+            )
+        )
+    ]
     barrier = pltpu.get_barrier_semaphore()
 
     def greet(step, carry):
@@ -73,6 +94,8 @@
         return carry
 
     lax.fori_loop(1, count, greet, 0)
+    for load in loads:
+        load.start()
 
     def normalize(source, gain, target):
         def chunk(index, carry):
@@ -101,15 +124,25 @@
             return carry
 
         lax.fori_loop(0, count - 1, one, 0)
+
+    def keep(source, target):
         target[pl.ds(first_row, rows), :] = source[:, columns_of(me)]
 
     triples = ((0, v_ref, all_v), (1, norm_k, all_k), (2, norm_q, all_q))
-    normalize(k_ref, key_gain, norm_k)
     pl.semaphore_wait(barrier, count - 1)
     send(*triples[0])
+    loads[0].wait()
+    loads[1].wait()
+    normalize(k_ref, key_gain, norm_k)
     send(*triples[1])
+    loads[2].wait()
+    loads[3].wait()
     normalize(q_ref, query_gain, norm_q)
     send(*triples[2])
+    keep(norm_k, all_k)
+    keep(norm_q, all_q)
+    for load in loads[4:]:
+        load.wait()
 
     def outgoing(step):
         to_section, to_seq = peer(step)
@@ -213,14 +246,19 @@
     count = sections * seq_count
     own_heads = HEADS // count
     tokens = count * rows
-    vmem = pl.BlockSpec(memory_space=pltpu.VMEM)
-    smem = pl.BlockSpec(memory_space=pltpu.SMEM)
+    hbm = pl.BlockSpec(memory_space=pltpu.HBM)
     return pl.pallas_call(
         functools.partial(kernel, sections, seq_count),
         out_shape=jax.ShapeDtypeStruct((rows, width), jnp.bfloat16),
-        in_specs=[vmem, vmem, vmem, vmem, vmem, smem, smem],
+        in_specs=[hbm] * 7,
         out_specs=pl.BlockSpec(memory_space=pl.ANY),
         scratch_shapes=[
+            pltpu.VMEM((rows, width), jnp.bfloat16),
+            pltpu.VMEM((rows, width), jnp.bfloat16),
+            pltpu.VMEM((1, width), jnp.float32),
+            pltpu.VMEM((1, width), jnp.float32),
+            pltpu.SMEM(placement.shape, jnp.int32),
+            pltpu.SMEM(span_mask.shape, jnp.int32),
             pltpu.VMEM((rows, width), jnp.bfloat16),
             pltpu.VMEM((rows, width), jnp.bfloat16),
             pltpu.VMEM((tokens, own_heads * HEAD_DIM), jnp.bfloat16),
@@ -232,9 +270,10 @@
             pltpu.SemaphoreType.DMA((count,)),
             pltpu.SemaphoreType.DMA((count,)),
             pltpu.SemaphoreType.DMA,
+            pltpu.SemaphoreType.DMA((7,)),
         ],
         compiler_params=pltpu.CompilerParams(
-            collective_id=0, has_side_effects=True, vmem_limit_bytes=40 * 1024 * 1024
+            collective_id=0, has_side_effects=True, vmem_limit_bytes=64 * 1024 * 1024
         ),
     )(
         queries,

time: 60.2 us -> 55.7 us (0.925)
  local copies, waits for them, and re-layouts: 6.04 us -> 1.87 us
    unnamed x15 -> x1, local copies, waits for them, and re-layouts: 6.04 us -> 1.87 us
where the time goes in v3:
time: 55.7 us; the launch traced here: 55.6 us
  Pallas kernels  53.7 us (96%)
  local copies, waits for them, and re-layouts  1.87 us (3%)
    pallas_call x1, Pallas kernels, spread(): pl.pallas_call(functools.partial(kernel, sections, seq_count), out_shape=...  53.7 us
    unnamed x1, local copies, waits for them, and re-layouts  1.87 us

profile of v3, /device:TPU:0, one launch (start us, length us, event | category | flops | bytes accessed | tf_op | source)
XLA Modules:
  0.0 55.6 jit_solution(2353822986083094354)
XLA Ops:
  0.0 53.7 %shard_map.73 = bf16[64,4096]{1,0:T(8,128)(2,1)} custom-call(bf16[64,4096]{1,0:T(8,128)(2,1)} %q_hbm.1, bf16[64,4096]{1,0:T(8,128)(2,1)} %k_hbm.1, bf16[64,4096]{1,0:T(8,128)(2,1)} %v_ref.1, f32[1,4096]{1,0:T(1,128)} %bitcast.2, f32[1,4096]{1,0:T(1,128)} %bitcast.3, s32[4]{0:T(128)} %placement_hbm.1, s32[4,4]{1,0:T(4,128)} %span_mask_hbm.1), custom_call_target="tpu_custom_call" | custom-call | tf_op jit(solution)/shard_map/pallas_call | solution.py:250
  53.7 1.9 %copy.9 = bf16[64,4096]{1,0:T(8,128)(2,1)} copy(bf16[64,4096]{1,0:T(8,128)(2,1)} %shard_map.73) | data formatting | bytes 1048576

commit v4 on v3

--- a/solution.py
+++ b/solution.py
@@ -249,7 +249,7 @@
     hbm = pl.BlockSpec(memory_space=pltpu.HBM)
     return pl.pallas_call(
         functools.partial(kernel, sections, seq_count),
-        out_shape=jax.ShapeDtypeStruct((rows, width), jnp.bfloat16),
+        out_shape=pltpu.VMEM((rows, width), jnp.bfloat16),
         in_specs=[hbm] * 7,
         out_specs=pl.BlockSpec(memory_space=pl.ANY),
         scratch_shapes=[
@@ -273,7 +273,7 @@
             pltpu.SemaphoreType.DMA((7,)),
         ],
         compiler_params=pltpu.CompilerParams(
-            collective_id=0, has_side_effects=True, vmem_limit_bytes=64 * 1024 * 1024
+            collective_id=0, has_side_effects=True, vmem_limit_bytes=55 * 1024 * 1024
         ),
     )(
         queries,

time: 55.7 us -> 54.5 us (0.978)
  local copies, waits for them, and re-layouts: 1.87 us -> 0.8 us
    unnamed x1, local copies, waits for them, and re-layouts: 1.87 us -> 0.8 us
where the time goes in v4:
time: 54.5 us; the launch traced here: 54.4 us
  Pallas kernels  53.6 us (98%)
  local copies, waits for them, and re-layouts  0.8 us (1%)
    pallas_call x1, Pallas kernels, spread(): pl.pallas_call(functools.partial(kernel, sections, seq_count), out_shape=...  53.6 us

profile of v4, /device:TPU:0, one launch (start us, length us, event | category | flops | bytes accessed | tf_op | source)
XLA Modules:
  0.0 54.4 jit_solution(14961813358811700768)
XLA Ops:
  0.0 53.6 %shard_map.73 = bf16[64,4096]{1,0:T(8,128)(2,1)S(1)} custom-call(bf16[64,4096]{1,0:T(8,128)(2,1)} %q_hbm.1, bf16[64,4096]{1,0:T(8,128)(2,1)} %k_hbm.1, bf16[64,4096]{1,0:T(8,128)(2,1)} %v_ref.1, f32[1,4096]{1,0:T(1,128)} %bitcast.2, f32[1,4096]{1,0:T(1,128)} %bitcast.3, s32[4]{0:T(128)} %placement_hbm.1, s32[4,4]{1,0:T(4,128)} %span_mask_hbm.1), custom_call_target="tpu_custom_call" | custom-call | tf_op jit(solution)/shard_map/pallas_call | solution.py:250
  53.6 0.8 %copy.9 = bf16[64,4096]{1,0:T(8,128)(2,1)} copy(bf16[64,4096]{1,0:T(8,128)(2,1)S(1)} %shard_map.73) | data formatting | bytes 1048576

commit v5 on v4

--- a/solution.py
+++ b/solution.py
@@ -120,7 +120,10 @@
 
     def send(which, source, target):
         def one(index, carry):
-            incoming(which, source, target, count - 1 - index).start()
+            half = count // 2
+            far = 1 - index // half
+            step = far * (half + index) + (1 - far) * (count - 1 - index)
+            incoming(which, source, target, step).start()
             return carry
 
         lax.fori_loop(0, count - 1, one, 0)
@@ -200,7 +203,9 @@
     lax.fori_loop(1, count, arrived, 0)
 
     def tile(index, carry):
-        flips = sections - 1 - index
+        half = max(sections // 2, 1)
+        far = 1 - index // half
+        flips = far * (half + index) + (1 - far) * (sections - 1 - index)
 
         def take(other, inner):
             step = flips * seq_count + other

time: 54.5 us -> 54.1 us (level)
  no operation moved by 1% of the time
where the time goes in v5:
time: 54.1 us; the launch traced here: 54 us
  Pallas kernels  53.2 us (98%)
  local copies, waits for them, and re-layouts  0.8 us (1%)
    pallas_call x1, Pallas kernels, spread(): pl.pallas_call(functools.partial(kernel, sections, seq_count), out_shape=...  53.2 us

profile of v5, /device:TPU:0, one launch (start us, length us, event | category | flops | bytes accessed | tf_op | source)
XLA Modules:
  0.0 54.0 jit_solution(13404068942966043473)
XLA Ops:
  0.0 53.2 %shard_map.73 = bf16[64,4096]{1,0:T(8,128)(2,1)S(1)} custom-call(bf16[64,4096]{1,0:T(8,128)(2,1)} %q_hbm.1, bf16[64,4096]{1,0:T(8,128)(2,1)} %k_hbm.1, bf16[64,4096]{1,0:T(8,128)(2,1)} %v_ref.1, f32[1,4096]{1,0:T(1,128)} %bitcast.2, f32[1,4096]{1,0:T(1,128)} %bitcast.3, s32[4]{0:T(128)} %placement_hbm.1, s32[4,4]{1,0:T(4,128)} %span_mask_hbm.1), custom_call_target="tpu_custom_call" | custom-call | tf_op jit(solution)/shard_map/pallas_call | solution.py:255
  53.2 0.8 %copy.9 = bf16[64,4096]{1,0:T(8,128)(2,1)} copy(bf16[64,4096]{1,0:T(8,128)(2,1)S(1)} %shard_map.73) | data formatting | bytes 1048576

commit v6 on v5

--- a/solution.py
+++ b/solution.py
@@ -93,7 +93,8 @@
         )
         return carry
 
-    lax.fori_loop(1, count, greet, 0)
+    for step in range(count - 1, 0, -1):
+        greet(step, 0)
     for load in loads:
         load.start()
 

time: 54.1 us -> 54.1 us (level)
  no operation moved by 1% of the time
where the time goes in v6:
time: 54.1 us; the launch traced here: 53.9 us
  Pallas kernels  53.1 us (98%)
  local copies, waits for them, and re-layouts  0.8 us (1%)
    pallas_call x1, Pallas kernels, spread(): pl.pallas_call(functools.partial(kernel, sections, seq_count), out_shape=...  53.1 us

profile of v6, /device:TPU:0, one launch (start us, length us, event | category | flops | bytes accessed | tf_op | source)
XLA Modules:
  0.0 53.9 jit_solution(17683859685578621619)
XLA Ops:
  0.0 53.1 %shard_map.73 = bf16[64,4096]{1,0:T(8,128)(2,1)S(1)} custom-call(bf16[64,4096]{1,0:T(8,128)(2,1)} %q_hbm.1, bf16[64,4096]{1,0:T(8,128)(2,1)} %k_hbm.1, bf16[64,4096]{1,0:T(8,128)(2,1)} %v_ref.1, f32[1,4096]{1,0:T(1,128)} %bitcast.2, f32[1,4096]{1,0:T(1,128)} %bitcast.3, s32[4]{0:T(128)} %placement_hbm.1, s32[4,4]{1,0:T(4,128)} %span_mask_hbm.1), custom_call_target="tpu_custom_call" | custom-call | tf_op jit(solution)/shard_map/pallas_call | solution.py:256
  53.1 0.8 %copy.9 = bf16[64,4096]{1,0:T(8,128)(2,1)} copy(bf16[64,4096]{1,0:T(8,128)(2,1)S(1)} %shard_map.73) | data formatting | bytes 1048576
